TPU v7x, 32 devices: a whole 2x2x4 slice. The times are simulated.
32 devices in a mesh: date: 8 (over z, x), col: 4 (over y, core).
Axes of the slice: x: 2, y: 2, z: 4, core: 2. Of those that a mesh axis runs over, the one named last changes fastest.
Arguments:
- slc: float32 [2, 8, 32, 2048], P(None, 'date', None, 'col'), may hold values from -80 to 80
- offsets: int32 [8, 4], replicated, may hold values from 0 to 6, as said below
Outputs:
- interferogram: float32 [2, 8, 4, 8, 128], P(None, 'date', None, None, 'col')
- coherence: float32 [8, 4, 8, 128], P('date', None, None, 'col')
Inputs may be any that keep to these rules, and one draw needn't show every extreme that they name: Row d lists the offsets of the pairs whose reference date is d; 0 marks an empty slot, the nonzero entries of a row are distinct, and d plus each offset is at most 7. Date 0 has 4 pairs, one of offset 6.
All inputs are finite; a program needn't handle non-finite values.
Results may differ from a plain program's by a relative error of at most 0.0003.
Values sent between devices are 32-bit elements; how exact they have to be, the bound alone decides.
A program may use at most 64 MiB of HBM per device.

v0:
```python
import jax
import jax.numpy as jnp
from jax import lax
from jax.sharding import PartitionSpec as P

epsilon = 1e-06


def with_halo(cells, sides, width):
    for axis, dim in sides:
        count = lax.axis_size(axis)
        ends = count - 1
        head = lax.slice_in_dim(cells, 0, width, axis=dim)
        tail = lax.slice_in_dim(cells, cells.shape[dim] - width, cells.shape[dim], axis=dim)
        cells = jnp.concatenate(
            [
                lax.ppermute(tail, axis, [(i, (i + 1) % count) for i in range(ends)]),
                cells,
                lax.ppermute(head, axis, [((i + 1) % count, i) for i in range(ends)]),
            ],
            axis=dim,
        )
    return cells


def look_sums(master_real, master_imag, partner_real, partner_imag, live_mask):
    prod_real = master_real * partner_real + master_imag * partner_imag
    prod_imag = master_imag * partner_real - master_real * partner_imag
    power_master = master_real * master_real + master_imag * master_imag
    power_partner = partner_real * partner_real + partner_imag * partner_imag
    power_master = jnp.broadcast_to(power_master, prod_real.shape)
    stacked = jnp.stack([prod_real, prod_imag, power_master, power_partner])
    full_shape = stacked.shape
    blocks = stacked.reshape(full_shape[:-2] + (full_shape[-2] // 4, 4, full_shape[-1] // 16, 16))
    looked = jnp.sum(blocks, axis=(-3, -1)) / 64.0
    return looked * live_mask


def coherence_of(padded):
    row_count = padded.shape[-2] - 2
    col_count = padded.shape[-1] - 2
    window_sum = padded[..., 0:row_count, 0:col_count]
    for down_step in range(3):
        for side_step in range(3):
            if down_step or side_step:
                window_sum = (
                    window_sum
                    + padded[
                        ..., down_step : down_step + row_count, side_step : side_step + col_count
                    ]
                )
    magnitude = jnp.sqrt(window_sum[0] * window_sum[0] + window_sum[1] * window_sum[1])
    return magnitude / (jnp.sqrt(window_sum[2] * window_sum[3]) + epsilon)


def shards(slc, offsets):
    date_count = offsets.shape[0]
    slot_count = offsets.shape[1]
    blocks = lax.all_to_all(slc, "date", split_axis=2, concat_axis=1, tiled=True)
    block_rows = blocks.shape[2]
    col_width = blocks.shape[3]
    partner_index = jnp.clip(
        jnp.arange(date_count, dtype=jnp.int32)[:, None] + offsets, 0, date_count - 1
    )
    live_mask = (offsets > 0).astype(jnp.float32)
    partner = jnp.take(blocks, partner_index.reshape(-1), axis=1)
    partner = partner.reshape(2, date_count, slot_count, block_rows, col_width)
    local_sums = look_sums(
        blocks[0][:, None], blocks[1][:, None], partner[0], partner[1], live_mask[:, :, None, None]
    )
    looked = lax.all_to_all(local_sums, "date", split_axis=1, concat_axis=3, tiled=True)
    padded = with_halo(looked, (("col", 4),), 1)
    padded = jnp.pad(padded, ((0, 0), (0, 0), (0, 0), (1, 1), (0, 0)))
    return (looked[0:2], coherence_of(padded))


def solution(mesh):
    placed = (P(None, "date", None, "col"), P())
    return jax.shard_map(
        shards,
        mesh=mesh,
        in_specs=placed,
        out_specs=(P(None, "date", None, None, "col"), P("date", None, None, "col")),
        check_vma=False,
    )
```

profile of v0, /device:TPU:1, one launch (start us, length us, event | category | flops | bytes accessed | tf_op | source)
XLA Modules:
  0.0 46.0 jit_solution(209143733925910426)
XLA Ops:
  0.6 1.6 %copy.31 = f32[2,1,32,512]{3,0,1,2:T(2,128)} copy(f32[2,1,32,512]{3,2,1,0:T(8,128)} %param.2) | data formatting | bytes 262144 | tf_op args[0]
  2.3 6.4 %all-to-all-start = ((f32[2,1,32,512]{3,0,1,2:T(2,128)}), f32[2,1,32,512]{3,0,1,2:T(2,128)S(1)}, u32[]{:S(2)}, u32[]{:S(2)}) async-start(f32[2,1,32,512]{3,0,1,2:T(2,128)} %copy.31), calls=%async_computation | async-start | bytes 262144 | tf_op jit(solution)/shard_map/all_to_all | solution.py:59
  8.6 0.7 %add_clamp_fusion = s32[8,4]{0,1:T(4,128)S(1)} fusion(s32[8,4]{0,1:T(4,128)} %param.3), kind=kLoop, calls=%fused_computation.38 | loop fusion | flops 64 | bytes 256 | tf_op jit(solution)/shard_map/jit(clip)/min | solution.py:62
  9.3 0.7 %compare_select_fusion.2 = f32[8,4]{0,1:T(4,128)S(1)} fusion(s32[8,4]{0,1:T(4,128)} %param.3), kind=kLoop, calls=%fused_computation.39 | loop fusion | flops 64 | bytes 256 | tf_op jit(solution)/shard_map/mul | solution.py:36
  10.3 4.5 %all-to-all-done = f32[2,1,32,512]{3,0,1,2:T(2,128)S(1)} async-done(((f32[2,1,32,512]{3,0,1,2:T(2,128)}), f32[2,1,32,512]{3,0,1,2:T(2,128)S(1)}, u32[]{:S(2)}, u32[]{:S(2)}) %all-to-all-start) | async-done | bytes 131104 | tf_op jit(solution)/shard_map/all_to_all | solution.py:59
  14.9 0.9 %gather_fusion = f32[32,2,4,512]{3,2,1,0:T(4,128)S(1)} fusion(f32[2,8,4,512]{3,2,1,0:T(4,128)S(1)} %copy.44, s32[1024]{0:T(1024)S(1)} %pad_clamp_fusion), kind=kCustom, calls=%fused_computation | custom fusion | bytes 1048704 | tf_op jit(solution)/shard_map/jit(_take)/gather | solution.py:66
  15.7 0.2 select_bitcast_fusion
  16.0 0.1 copy.36
  16.1 0.7 %squeeze.4 = f32[1,8,4,1,4,32,16]{6,5,2,1,4,3,0:T(8,128)S(1)} reshape(f32[1,32,4,512]{3,1,2,0:T(8,128)S(1)} %copy.36) | data formatting | bytes 524288 | tf_op jit(solution)/shard_map/squeeze | solution.py:69
  16.8 0.1 copy.38
  16.9 2.1 %squeeze.5 = f32[1,8,4,1,4,32,16]{6,5,2,1,4,3,0:T(8,128)} reshape(f32[1,32,4,512]{3,1,2,0:T(8,128)S(1)} %copy.38) | data formatting | bytes 524288 | tf_op jit(solution)/shard_map/squeeze | solution.py:69
  19.0 0.3 slice_reduce_fusion.1
  19.3 0.2 mul.158
  19.5 0.2 mul.161
  19.7 0.1 multiply_add_fusion.2
  19.9 1.4 %copy-done = f32[1,8,4,1,4,32,16]{6,5,2,1,4,3,0:T(8,128)S(1)} copy-done((f32[1,8,4,1,4,32,16]{6,5,2,1,4,3,0:T(8,128)S(1)}, f32[1,8,4,1,4,32,16]{6,5,2,1,4,3,0:T(8,128)}, u32[]{:S(2)}) %copy-start) | copy-done | bytes 262168
  21.3 1.1 %multiply_add_fusion.1 = (f32[1,8,4,1,4,32,16]{6,5,2,1,4,3,0:T(8,128)S(1)}, f32[1,8,4,1,4,32,16]{6,5,2,1,4,3,0:T(8,128)S(1)}, f32[1,8,4,1,4,32,16]{6,5,2,1,4,3,0:T(8,128)S(1)}) fusion(f32[1,8,4,1,4,32,16]{6,5,2,1,4,3,0:T(8,128)S(1)} %copy-done, f32[1,8,4,1,4,32,16]{6,5,2,1,4,3,0:T(8,128)S(1)} %squeeze.4, f32[8,4,32,16]{3,2,1,0:T(8,128)S(1)} %mul.158, ...), kind=kLoop, calls=%fused_computation.4 | loop fusion | flops 589824 | bytes 1441792 | tf_op jit(solution)/shard_map/add | solution.py:27
  22.4 0.3 stack_broadcast_in_dim.2
  22.6 1.0 %maximum_reduce_fusion = f32[4,8,4,32]{3,2,1,0:T(4,128)S(1)} fusion(f32[1,8,4,1,4,32,16]{6,5,2,1,4,3,0:T(8,128)S(1)} %get-tuple-element.10, f32[1,8,4,1,4,32,16]{6,5,2,1,4,3,0:T(8,128)S(1)} %stack_broadcast_in_dim.2, f32[1,8,4,1,4,32,16]{6,5,2,1,4,3,0:T(8,128)S(1)} %get-tuple-element.9, f32[1,8,4,1,4,32,16]{6,5,2,1,4,3,0:T(8,128)S(1)} %get-tuple-element.8), kind=kLoop, calls=%fused_computation.1 | loop fusion | flops 1044480 | bytes 1064960 | tf_op jit(solution)/shard_map/reduce_sum | solution.py:35
  23.7 0.1 reshape.262
  23.8 7.8 %all_to_all.30 = f32[8,1,512]{2,1,0:T(1,128)S(1)} all-to-all(f32[8,1,512]{2,1,0:T(1,128)S(1)} %reshape.262), channel_id=1, replica_groups=mesh['date'=8,'col'=4] {'date'}, dimensions={0} | all-to-all | bytes 32768 | tf_op jit(solution)/shard_map/all_to_all | solution.py:71
  31.6 0.5 %broadcast.110 = f32[]{:T(128)} broadcast(f32[]{:T(128)} %constant.79), dimensions={} | broadcast | bytes 8 | tf_op jit(solution)/shard_map/all_to_all | solution.py:71
  32.1 0.7 %reduce.5 = f32[8,512]{1,0:T(8,128)S(1)} reduce(f32[8,1,512]{2,1,0:T(1,128)S(1)} %all_to_all.30, f32[]{:T(128)} %broadcast.110), dimensions={1}, to_apply=%all_to_all.24.reduce_sub_computation | reduce | bytes 32772 | tf_op jit(solution)/shard_map/all_to_all | solution.py:71
  32.8 0.1 reshape.263
  33.0 0.1 fusion.12
  33.1 6.3 %collective-permute-start = (f32[4,1,4,8,1]{4,2,0,3,1:T(4,128)S(1)}, f32[4,1,4,8,1]{4,2,0,3,1:T(4,128)S(1)}, u32[]{:S(2)}, u32[]{:S(2)}) collective-permute-start(f32[4,1,4,8,1]{4,2,0,3,1:T(4,128)S(1)} %get-tuple-element.13), channel_id=1, source_target_pairs={{0,1},{1,2},{2,3},{4,5},{5,6},{6,7},{8,9},{9,10},{10,11},{12,13},{... | collective-permute-start | bytes 1544 | tf_op jit(solution)/shard_map/ppermute | solution.py:17
  39.3 1.9 %collective-permute-start.1 = (f32[4,1,4,8,1]{4,2,0,3,1:T(4,128)S(1)}, f32[4,1,4,8,1]{4,2,0,3,1:T(4,128)S(1)}, u32[]{:S(2)}, u32[]{:S(2)}) collective-permute-start(f32[4,1,4,8,1]{4,2,0,3,1:T(4,128)S(1)} %get-tuple-element.14), channel_id=1, source_target_pairs={{1,0},{2,1},{3,2},{5,4},{6,5},{7,6},{9,8},{10,9},{11,10},{13,12},{... | collective-permute-start | bytes 1544 | tf_op jit(solution)/shard_map/ppermute | solution.py:19
  41.3 0.6 %copy.42 = f32[2,1,4,8,32]{4,3,2,1,0:T(8,128)} copy(f32[2,1,4,8,32]{4,2,0,3,1:T(4,128)S(1)} %slice_bitcast_fusion) | data formatting | bytes 16384
  41.9 3.0 %collective-permute-done.1 = f32[4,1,4,8,1]{4,2,0,3,1:T(4,128)S(1)} collective-permute-done((f32[4,1,4,8,1]{4,2,0,3,1:T(4,128)S(1)}, f32[4,1,4,8,1]{4,2,0,3,1:T(4,128)S(1)}, u32[]{:S(2)}, u32[]{:S(2)}) %collective-permute-start.1) | collective-permute-done | bytes 544 | tf_op jit(solution)/shard_map/ppermute | solution.py:19
  44.9 0.1 select_maximum_fusion
  45.1 0.3 slice_add_fusion
  45.4 0.6 %copy.43 = f32[1,4,8,32]{3,2,1,0:T(8,128)} copy(f32[1,4,8,32]{3,1,2,0:T(4,128)S(1)} %fusion.9) | data formatting | bytes 8192
  (17 shorter events, 0.6 us)
Async XLA Ops:
  2.3 12.6 %all-to-all-start = ((f32[2,1,32,512]{3,0,1,2:T(2,128)}), f32[2,1,32,512]{3,0,1,2:T(2,128)S(1)}, u32[]{:S(2)}, u32[]{:S(2)}) async-start(f32[2,1,32,512]{3,0,1,2:T(2,128)} %copy.31), calls=%async_computation | async-start | bytes 262144 | tf_op jit(solution)/shard_map/all_to_all | solution.py:59
  19.7 1.6 %copy-start = (f32[1,8,4,1,4,32,16]{6,5,2,1,4,3,0:T(8,128)S(1)}, f32[1,8,4,1,4,32,16]{6,5,2,1,4,3,0:T(8,128)}, u32[]{:S(2)}) copy-start(f32[1,8,4,1,4,32,16]{6,5,2,1,4,3,0:T(8,128)} %squeeze.5) | copy-start | bytes 786436
  33.1 8.8 %collective-permute-start = (f32[4,1,4,8,1]{4,2,0,3,1:T(4,128)S(1)}, f32[4,1,4,8,1]{4,2,0,3,1:T(4,128)S(1)}, u32[]{:S(2)}, u32[]{:S(2)}) collective-permute-start(f32[4,1,4,8,1]{4,2,0,3,1:T(4,128)S(1)} %get-tuple-element.13), channel_id=1, source_target_pairs={{0,1},{1,2},{2,3},{4,5},{5,6},{6,7},{8,9},{9,10},{10,11},{12,13},{... | collective-permute-start | bytes 1544 | tf_op jit(solution)/shard_map/ppermute | solution.py:17
  39.3 5.6 %collective-permute-start.1 = (f32[4,1,4,8,1]{4,2,0,3,1:T(4,128)S(1)}, f32[4,1,4,8,1]{4,2,0,3,1:T(4,128)S(1)}, u32[]{:S(2)}, u32[]{:S(2)}) collective-permute-start(f32[4,1,4,8,1]{4,2,0,3,1:T(4,128)S(1)} %get-tuple-element.14), channel_id=1, source_target_pairs={{1,0},{2,1},{3,2},{5,4},{6,5},{7,6},{9,8},{10,9},{11,10},{13,12},{... | collective-permute-start | bytes 1544 | tf_op jit(solution)/shard_map/ppermute | solution.py:19
where the time goes:
time: 46.4 us; the launch traced here: 46 us
  starting transfers between devices  14.5 us (31%)
  local copies, waits for them, and re-layouts  10.4 us (22%)
  blocking collectives  7.79 us (17%)
  waiting for transfers between devices  7.51 us (16%)
  other arithmetic  4.96 us (11%)
  between operations  0.84 us (2%)
    all_to_all x1, blocking collectives, shards(): lax.all_to_all(local_sums, 'date', split_axis=1, concat_axis=3, tiled=True)  7.79 us
    all_to_all x1, starting transfers between devices, shards(): lax.all_to_all(slc, 'date', split_axis=2, concat_axis=1, tiled=True)  6.35 us
    ppermute x1, starting transfers between devices, with_halo(): lax.ppermute(tail, axis, [(i, (i + 1) % count) for i in range(ends)])  6.27 us
    unnamed x7, local copies, waits for them, and re-layouts  4.52 us
    all_to_all x1, waiting for transfers between devices, shards(): lax.all_to_all(slc, 'date', split_axis=2, concat_axis=1, tiled=True)  4.49 us
    ppermute x1, waiting for transfers between devices, with_halo(): lax.ppermute(head, axis, [((i + 1) % count, i) for i in range(ends)])  3.02 us
    squeeze x1, local copies, waits for them, and re-layouts, shards(): partner[1]  2.07 us
    ppermute x1, starting transfers between devices, with_halo(): lax.ppermute(head, axis, [((i + 1) % count, i) for i in range(ends)])  1.92 us
  transfers between devices with their start and end apart: 3, of which 2 were waited for; matrix products, arithmetic and copies ran while one was open for 5% of the time, Pallas kernels for 0%

commit v1 on v0

v1 whole, which is shorter than its diff:
```python
import functools

import jax
import jax.numpy as jnp
from jax import lax
from jax.experimental import pallas as pl
from jax.experimental.pallas import tpu as pltpu
from jax.sharding import PartitionSpec as P

EPSILON = 1e-06
MAX_OFFSET = 6
LOOK_ROWS = 4
LOOK_COLS = 16
TILE = 8
LANES = 128
MESH = pl.DeviceIdType.MESH


def drain(ref, sem):
    pltpu.make_async_copy(ref, ref, sem).wait()


def split_dot(values, pool):
    total = None
    for _ in range(3):
        part = values.astype(jnp.bfloat16)
        values = values - part.astype(jnp.float32)
        dot = jnp.dot(part, pool, preferred_element_type=jnp.float32)
        total = dot if total is None else total + dot
    return total


def kernel(dates, cols, slots, slc, offsets, ifg, coh, blocks, offs, outbox, landed, halo, sems):
    date, col = lax.axis_index("date"), lax.axis_index("col")
    chunks = blocks.shape[1]
    width = chunks * LANES
    halves = slc.shape[2] // chunks
    cells = slc.shape[2] * LANES // LOOK_COLS
    rt, half = date // halves, date % halves
    side = lax.rem(col + cols + 2 * half - 1, cols)

    offs_copy = pltpu.make_async_copy(offsets, offs, sems.at[4])
    offs_copy.start()

    def tile_of(peer):
        return slc.at[:, peer // halves, pl.ds((peer % halves) * chunks, chunks)]

    my_rows = pl.ds(pl.multiple_of(date * TILE, TILE), TILE)
    pltpu.make_async_copy(tile_of(date), blocks.at[:, :, my_rows], sems.at[1]).start()

    barrier = pltpu.get_barrier_semaphore()
    for step in range(1, dates):
        peer = lax.rem(date + step, dates)
        pl.semaphore_signal(barrier, inc=1, device_id=(peer, col), device_id_type=MESH)
    for step in (1, cols - 1):
        other = lax.rem(col + step, cols)
        pl.semaphore_signal(barrier, inc=1, device_id=(date, other), device_id_type=MESH)
    pl.semaphore_wait(barrier, dates + 1)

    for step in range(1, dates):
        peer = lax.rem(date + step, dates)
        pltpu.make_async_remote_copy(
            src_ref=tile_of(peer),
            dst_ref=blocks.at[:, :, my_rows],
            send_sem=sems.at[0],
            recv_sem=sems.at[1],
            device_id=(peer, col),
            device_id_type=MESH,
        ).start()

    looked_col = lax.broadcasted_iota(jnp.int32, (width, LANES), 0) // LOOK_COLS
    per_half = width // LOOK_COLS
    shown = lax.broadcasted_iota(jnp.int32, (width, LANES), 1) % per_half
    pool = jnp.where(looked_col == shown, 1.0 / (LOOK_ROWS * LOOK_COLS), 0.0).astype(jnp.bfloat16)
    lane = lax.broadcasted_iota(jnp.int32, (dates, LANES), 1)
    offs_copy.wait()
    lane_off = jnp.zeros((dates, LANES), jnp.int32)
    for slot in range(slots):
        mine = (lane // cells == slot) & ((lane % cells) // per_half == half)
        lane_off = jnp.where(mine, offs[:, slot : slot + 1], lane_off)
    chosen = [lane_off == o for o in range(1, MAX_OFFSET + 1)]

    drain(blocks, sems.at[1])

    look_count = TILE // LOOK_ROWS
    pieces = []
    for look in range(look_count):
        real_sums = [None] * MAX_OFFSET
        imag_sums = [None] * MAX_OFFSET
        power = None
        for row in range(look * LOOK_ROWS, (look + 1) * LOOK_ROWS):
            a0, a1 = [
                jnp.concatenate(
                    [
                        blocks[comp, chunk, pl.ds(row, dates, stride=TILE), :]
                        for chunk in range(chunks)
                    ],
                    axis=1,
                )
                for comp in range(2)
            ]
            squares = a0 * a0 + a1 * a1
            power = squares if power is None else power + squares
            for o in range(1, MAX_OFFSET + 1):
                b0 = pltpu.roll(a0, dates - o, 0)
                b1 = pltpu.roll(a1, dates - o, 0)
                real = a0 * b0 + a1 * b1
                imag = a1 * b0 - a0 * b1
                real_sums[o - 1] = real if real_sums[o - 1] is None else real_sums[o - 1] + real
                imag_sums[o - 1] = imag if imag_sums[o - 1] is None else imag_sums[o - 1] + imag
        pieces += real_sums + imag_sums + [power]
    pooled = split_dot(jnp.concatenate(pieces, axis=0), pool)

    count = 2 * MAX_OFFSET + 1
    for look in range(look_count):
        part = [
            pooled[(look * count + q) * dates : (look * count + q + 1) * dates] for q in range(count)
        ]
        planes = [jnp.zeros((dates, LANES), jnp.float32) for _ in range(4)]
        for o in range(1, MAX_OFFSET + 1):
            take = chosen[o - 1]
            planes[0] = jnp.where(take, part[o - 1], planes[0])
            planes[1] = jnp.where(take, part[MAX_OFFSET + o - 1], planes[1])
            planes[2] = jnp.where(take, part[2 * MAX_OFFSET], planes[2])
            planes[3] = jnp.where(take, pltpu.roll(part[2 * MAX_OFFSET], dates - o, 0), planes[3])
        for k in range(4):
            outbox[pl.ds(look * 4 + k, dates, stride=TILE), :] = planes[k]

    spot = pl.ds(pl.multiple_of(rt * TILE, TILE), TILE)
    for step in range(dates):
        peer = lax.rem(date + step, dates)
        tile = outbox.at[pl.ds(pl.multiple_of(peer * TILE, TILE), TILE)]
        if step:
            pltpu.make_async_remote_copy(
                src_ref=tile,
                dst_ref=landed.at[half, spot],
                send_sem=sems.at[2],
                recv_sem=sems.at[3],
                device_id=(peer, col),
                device_id_type=MESH,
            ).start()
        else:
            pltpu.make_async_copy(tile, landed.at[half, spot], sems.at[3]).start()
        pltpu.make_async_remote_copy(
            src_ref=tile,
            dst_ref=halo.at[half, spot],
            send_sem=sems.at[5],
            recv_sem=sems.at[6],
            device_id=(peer, side),
            device_id_type=MESH,
        ).start()

    look_rows = landed.shape[1] // 4
    lane = lax.broadcasted_iota(jnp.int32, (look_rows, LANES), 1) % cells
    line = lax.broadcasted_iota(jnp.int32, (look_rows, LANES), 0)
    left_edge, right_edge = lane == 0, lane == cells - 1
    has_left = jnp.where(col > 0, 1.0, 0.0)
    has_right = jnp.where(col < cols - 1, 1.0, 0.0)

    drain(landed, sems.at[3])
    drain(halo, sems.at[6])
    sums = []
    for k in range(4):
        plane = pl.ds(k, look_rows, stride=4)
        main = landed[0, plane, :]
        for other in range(1, halves):
            main = main + landed[other, plane, :]
        if k < 2:
            for slot in range(slots):
                ifg[k, 0, slot] = main[:, slot * cells : (slot + 1) * cells]
        after = pltpu.roll(halo[0, plane, :], cells - 1, 1) * has_right
        before = pltpu.roll(halo[halves - 1, plane, :], LANES - (cells - 1), 1) * has_left
        right = jnp.where(right_edge, after, pltpu.roll(main, LANES - 1, 1))
        left = jnp.where(left_edge, before, pltpu.roll(main, 1, 1))
        wide = main + left + right
        up = jnp.where(line == 0, 0.0, pltpu.roll(wide, 1, 0))
        down = jnp.where(line == look_rows - 1, 0.0, pltpu.roll(wide, look_rows - 1, 0))
        sums.append(wide + up + down)
    magnitude = jnp.sqrt(sums[0] * sums[0] + sums[1] * sums[1])
    result = magnitude / (jnp.sqrt(sums[2] * sums[3]) + EPSILON)
    for slot in range(slots):
        coh[0, slot] = result[:, slot * cells : (slot + 1) * cells]

    drain(blocks.at[:, :, pl.ds(0, (dates - 1) * TILE)], sems.at[0])
    drain(outbox.at[pl.ds(0, (dates - 1) * TILE)], sems.at[2])
    drain(outbox, sems.at[5])


def solution(mesh):
    dates, cols = mesh.shape["date"], mesh.shape["col"]

    def shards(slc, offsets):
        rows, columns = slc.shape[2], slc.shape[3]
        slots = offsets.shape[1]
        row_tiles = rows // TILE
        halves = dates // row_tiles
        if halves != 2 or slots * columns // LOOK_COLS != LANES:
            raise ValueError("unsupported sizes")
        width = columns // halves
        look_rows, cells = rows // LOOK_ROWS, columns // LOOK_COLS
        tiles = slc.reshape(2, row_tiles, TILE, columns // LANES, LANES).transpose(0, 1, 3, 2, 4)
        return tuple(
            pl.pallas_call(
                functools.partial(kernel, dates, cols, slots),
                out_shape=(
                    jax.ShapeDtypeStruct((2, 1, slots, look_rows, cells), jnp.float32),
                    jax.ShapeDtypeStruct((1, slots, look_rows, cells), jnp.float32),
                ),
                in_specs=[pl.BlockSpec(memory_space=pl.ANY)] * 2,
                out_specs=(pl.BlockSpec(memory_space=pltpu.VMEM),) * 2,
                scratch_shapes=[
                    pltpu.VMEM((2, width // LANES, dates * TILE, LANES), jnp.float32),
                    pltpu.VMEM(offsets.shape, jnp.int32),
                    pltpu.VMEM((dates * TILE, LANES), jnp.float32),
                    pltpu.VMEM((halves, row_tiles * TILE, LANES), jnp.float32),
                    pltpu.VMEM((halves, row_tiles * TILE, LANES), jnp.float32),
                    pltpu.SemaphoreType.DMA((7,)),
                ],
                compiler_params=pltpu.CompilerParams(
                    collective_id=0, has_side_effects=True, vmem_limit_bytes=16 * 1024 * 1024
                ),
            )(tiles, offsets)
        )

    return jax.shard_map(
        shards,
        mesh=mesh,
        in_specs=(P(None, "date", None, "col"), P()),
        out_specs=(P(None, "date", None, None, "col"), P("date", None, None, "col")),
        check_vma=False,
    )
```

time: 46.4 us -> 19.4 us (0.42)
  the two profiles are of different devices: /device:TPU:1 before, /device:TPU:0 now
where the time goes in v1:
time: 19.4 us; the launch traced here: 19.2 us
  Pallas kernels  15.7 us (81%)
  local copies, waits for them, and re-layouts  2.88 us (15%)
  between operations  0.64 us (3%)
    pallas_call x1, Pallas kernels, shards(): pl.pallas_call(functools.partial(kernel, dates, cols, slots), out_shape=(...  15.7 us
    unnamed x5, local copies, waits for them, and re-layouts  2.88 us

profile of v1, /device:TPU:0, one launch (start us, length us, event | category | flops | bytes accessed | tf_op | source)
XLA Modules:
  0.0 19.2 jit_solution(15581542475049694443)
XLA Ops:
  0.6 0.8 %copy.4.offsets = s32[8,4]{1,0:T(8,128)S(1)} copy(s32[8,4]{0,1:T(4,128)} %param.3) | data formatting | bytes 256 | tf_op args[1]
  1.4 0.0 copy-start
  1.4 0.9 %copy-done = f32[2,1,32,512]{3,2,1,0:T(8,128)S(1)} copy-done((f32[2,1,32,512]{3,2,1,0:T(8,128)S(1)}, f32[2,1,32,512]{3,2,1,0:T(8,128)}, u32[]{:S(2)}) %copy-start) | copy-done | bytes 131096
  2.3 15.7 %shard_map.41 = (f32[2,1,4,8,32]{4,3,2,1,0:T(8,128)S(1)}, f32[1,4,8,32]{3,2,1,0:T(8,128)S(1)}) custom-call(f32[2,4,4,8,128]{4,3,2,1,0:T(8,128)S(1)} %bitcast.3, s32[8,4]{1,0:T(8,128)S(1)} %copy.4.offsets), custom_call_target="tpu_custom_call" | custom-call | tf_op jit(solution)/shard_map/pallas_call | solution.py:203
  18.0 0.6 %copy.7 = f32[2,1,4,8,32]{4,3,2,1,0:T(8,128)} copy(f32[2,1,4,8,32]{4,3,2,1,0:T(8,128)S(1)} %get-tuple-element.4) | data formatting | bytes 16384
  18.6 0.6 %copy.8 = f32[1,4,8,32]{3,2,1,0:T(8,128)} copy(f32[1,4,8,32]{3,2,1,0:T(8,128)S(1)} %get-tuple-element.5) | data formatting | bytes 8192
Async XLA Ops:
  1.4 0.9 %copy-start = (f32[2,1,32,512]{3,2,1,0:T(8,128)S(1)}, f32[2,1,32,512]{3,2,1,0:T(8,128)}, u32[]{:S(2)}) copy-start(f32[2,1,32,512]{3,2,1,0:T(8,128)} %param.2) | copy-start | bytes 393220

commit v2 on v1

--- a/solution.py
+++ b/solution.py
@@ -30,7 +30,7 @@
     return total
 
 
-def kernel(dates, cols, slots, slc, offsets, ifg, coh, blocks, offs, outbox, landed, halo, sems):
+def kernel(dates, cols, slots, slc, offsets, dense, blocks, offs, outbox, landed, halo, sems):
     date, col = lax.axis_index("date"), lax.axis_index("col")
     chunks = blocks.shape[1]
     width = chunks * LANES
@@ -38,6 +38,8 @@
     cells = slc.shape[2] * LANES // LOOK_COLS
     rt, half = date // halves, date % halves
     side = lax.rem(col + cols + 2 * half - 1, cols)
+
+    order = sorted(range(1, dates), key=lambda step: abs(2 * step - dates))
 
     offs_copy = pltpu.make_async_copy(offsets, offs, sems.at[4])
     offs_copy.start()
@@ -57,7 +59,7 @@
         pl.semaphore_signal(barrier, inc=1, device_id=(date, other), device_id_type=MESH)
     pl.semaphore_wait(barrier, dates + 1)
 
-    for step in range(1, dates):
+    for step in order:
         peer = lax.rem(date + step, dates)
         pltpu.make_async_remote_copy(
             src_ref=tile_of(peer),
@@ -75,9 +77,14 @@
     lane = lax.broadcasted_iota(jnp.int32, (dates, LANES), 1)
     offs_copy.wait()
     lane_off = jnp.zeros((dates, LANES), jnp.int32)
+    eye = lax.broadcasted_iota(jnp.int32, (dates, dates), 0) == lax.broadcasted_iota(
+        jnp.int32, (dates, dates), 1
+    )
     for slot in range(slots):
+        row = offs[slot : slot + 1, :].astype(jnp.float32)
+        column = jnp.sum(jnp.where(eye, row, 0.0), axis=1, keepdims=True).astype(jnp.int32)
         mine = (lane // cells == slot) & ((lane % cells) // per_half == half)
-        lane_off = jnp.where(mine, offs[:, slot : slot + 1], lane_off)
+        lane_off = jnp.where(mine, column, lane_off)
     chosen = [lane_off == o for o in range(1, MAX_OFFSET + 1)]
 
     drain(blocks, sems.at[1])
@@ -127,7 +134,7 @@
             outbox[pl.ds(look * 4 + k, dates, stride=TILE), :] = planes[k]
 
     spot = pl.ds(pl.multiple_of(rt * TILE, TILE), TILE)
-    for step in range(dates):
+    for step in order + [0]:
         peer = lax.rem(date + step, dates)
         tile = outbox.at[pl.ds(pl.multiple_of(peer * TILE, TILE), TILE)]
         if step:
@@ -166,8 +173,7 @@
         for other in range(1, halves):
             main = main + landed[other, plane, :]
         if k < 2:
-            for slot in range(slots):
-                ifg[k, 0, slot] = main[:, slot * cells : (slot + 1) * cells]
+            dense[k] = main
         after = pltpu.roll(halo[0, plane, :], cells - 1, 1) * has_right
         before = pltpu.roll(halo[halves - 1, plane, :], LANES - (cells - 1), 1) * has_left
         right = jnp.where(right_edge, after, pltpu.roll(main, LANES - 1, 1))
@@ -177,13 +183,20 @@
         down = jnp.where(line == look_rows - 1, 0.0, pltpu.roll(wide, look_rows - 1, 0))
         sums.append(wide + up + down)
     magnitude = jnp.sqrt(sums[0] * sums[0] + sums[1] * sums[1])
-    result = magnitude / (jnp.sqrt(sums[2] * sums[3]) + EPSILON)
-    for slot in range(slots):
-        coh[0, slot] = result[:, slot * cells : (slot + 1) * cells]
+    dense[2] = magnitude / (jnp.sqrt(sums[2] * sums[3]) + EPSILON)
 
     drain(blocks.at[:, :, pl.ds(0, (dates - 1) * TILE)], sems.at[0])
     drain(outbox.at[pl.ds(0, (dates - 1) * TILE)], sems.at[2])
     drain(outbox, sems.at[5])
+
+
+def spread(slots, dense, ifg, coh):
+    cells = ifg.shape[-1]
+    for slot in range(slots):
+        part = slice(slot * cells, (slot + 1) * cells)
+        ifg[0, 0, slot] = dense[0, :, part]
+        ifg[1, 0, slot] = dense[1, :, part]
+        coh[0, slot] = dense[2, :, part]
 
 
 def solution(mesh):
@@ -199,27 +212,31 @@
         width = columns // halves
         look_rows, cells = rows // LOOK_ROWS, columns // LOOK_COLS
         tiles = slc.reshape(2, row_tiles, TILE, columns // LANES, LANES).transpose(0, 1, 3, 2, 4)
+        dense = pl.pallas_call(
+            functools.partial(kernel, dates, cols, slots),
+            out_shape=jax.ShapeDtypeStruct((3, look_rows, LANES), jnp.float32),
+            in_specs=[pl.BlockSpec(memory_space=pltpu.HBM)] * 2,
+            out_specs=pl.BlockSpec(memory_space=pltpu.VMEM),
+            scratch_shapes=[
+                pltpu.VMEM((2, width // LANES, dates * TILE, LANES), jnp.float32),
+                pltpu.VMEM((slots, dates), jnp.int32),
+                pltpu.VMEM((dates * TILE, LANES), jnp.float32),
+                pltpu.VMEM((halves, row_tiles * TILE, LANES), jnp.float32),
+                pltpu.VMEM((halves, row_tiles * TILE, LANES), jnp.float32),
+                pltpu.SemaphoreType.DMA((7,)),
+            ],
+            compiler_params=pltpu.CompilerParams(
+                collective_id=0, has_side_effects=True, vmem_limit_bytes=55104 * 1024
+            ),
+        )(tiles, offsets.T)
         return tuple(
             pl.pallas_call(
-                functools.partial(kernel, dates, cols, slots),
+                functools.partial(spread, slots),
                 out_shape=(
                     jax.ShapeDtypeStruct((2, 1, slots, look_rows, cells), jnp.float32),
                     jax.ShapeDtypeStruct((1, slots, look_rows, cells), jnp.float32),
                 ),
-                in_specs=[pl.BlockSpec(memory_space=pl.ANY)] * 2,
-                out_specs=(pl.BlockSpec(memory_space=pltpu.VMEM),) * 2,
-                scratch_shapes=[
-                    pltpu.VMEM((2, width // LANES, dates * TILE, LANES), jnp.float32),
-                    pltpu.VMEM(offsets.shape, jnp.int32),
-                    pltpu.VMEM((dates * TILE, LANES), jnp.float32),
-                    pltpu.VMEM((halves, row_tiles * TILE, LANES), jnp.float32),
-                    pltpu.VMEM((halves, row_tiles * TILE, LANES), jnp.float32),
-                    pltpu.SemaphoreType.DMA((7,)),
-                ],
-                compiler_params=pltpu.CompilerParams(
-                    collective_id=0, has_side_effects=True, vmem_limit_bytes=16 * 1024 * 1024
-                ),
-            )(tiles, offsets)
+            )(dense)
         )
 
     return jax.shard_map(

time: 19.4 us -> 19.6 us (1.010)
  Pallas kernels: 15.7 us -> 17.5 us
  local copies, waits for them, and re-layouts: 2.88 us -> 1.27 us
    pallas_call x1 -> x2, Pallas kernels: 15.7 us -> 17.5 us  [the longest x1 16.1 us: shards(): pl.pallas_call(functools.partial(kernel, dates, cols, slots), out_shape=j...]
    unnamed x5 -> x4, local copies, waits for them, and re-layouts: 2.88 us -> 1.27 us
where the time goes in v2:
time: 19.6 us; the launch traced here: 19.4 us
  Pallas kernels  17.5 us (89%)
  local copies, waits for them, and re-layouts  1.27 us (6%)
  between operations  0.65 us (3%)
    pallas_call x1, Pallas kernels, shards(): pl.pallas_call(functools.partial(kernel, dates, cols, slots), out_shape=j...  16.1 us
    pallas_call x1, Pallas kernels, shards(): pl.pallas_call(functools.partial(spread, slots), out_shape=(jax.ShapeDtyp...  1.4 us
    unnamed x4, local copies, waits for them, and re-layouts  1.27 us

profile of v2, /device:TPU:0, one launch (start us, length us, event | category | flops | bytes accessed | tf_op | source)
XLA Modules:
  0.0 19.4 jit_solution(15426759341851119823)
XLA Ops:
  0.6 0.0 copy-start.1
  0.6 0.7 %copy-done.1 = s32[8,4]{0,1:T(4,128)S(1)} copy-done((s32[8,4]{0,1:T(4,128)S(1)}, s32[8,4]{0,1:T(4,128)}, u32[]{:S(2)}) %copy-start.1) | copy-done | bytes 152
  1.3 16.1 %shard_map.41.dense = f32[3,8,128]{2,1,0:T(8,128)S(1)} custom-call(f32[2,4,4,8,128]{4,3,2,1,0:T(8,128)} %bitcast.5, s32[4,8]{1,0:T(4,128)S(1)} %bitcast.4), custom_call_target="tpu_custom_call" | custom-call | tf_op jit(solution)/shard_map/pallas_call | solution.py:215
  17.4 0.0 copy-start
  17.4 0.6 %copy-done = f32[3,8,128]{2,1,0:T(8,128)} copy-done((f32[3,8,128]{2,1,0:T(8,128)}, f32[3,8,128]{2,1,0:T(8,128)S(1)}, u32[]{:S(2)}) %copy-start) | copy-done | bytes 12312
  18.0 1.4 %shard_map.42 = (f32[2,1,4,8,32]{4,3,2,1,0:T(8,128)}, f32[1,4,8,32]{3,2,1,0:T(8,128)}) custom-call(f32[3,8,128]{2,1,0:T(8,128)} %copy-done), custom_call_target="tpu_custom_call" | custom-call | tf_op jit(solution)/shard_map/pallas_call | solution.py:233
Async XLA Ops:
  0.6 0.7 %copy-start.1 = (s32[8,4]{0,1:T(4,128)S(1)}, s32[8,4]{0,1:T(4,128)}, u32[]{:S(2)}) copy-start(s32[8,4]{0,1:T(4,128)} %param.3) | copy-start | bytes 388
  17.4 0.6 %copy-start = (f32[3,8,128]{2,1,0:T(8,128)}, f32[3,8,128]{2,1,0:T(8,128)S(1)}, u32[]{:S(2)}) copy-start(f32[3,8,128]{2,1,0:T(8,128)S(1)} %shard_map.41.dense) | copy-start | bytes 36868

commit v3 on v2

--- a/solution.py
+++ b/solution.py
@@ -44,11 +44,14 @@
     offs_copy = pltpu.make_async_copy(offsets, offs, sems.at[4])
     offs_copy.start()
 
-    def tile_of(peer):
-        return slc.at[:, peer // halves, pl.ds((peer % halves) * chunks, chunks)]
+    def tile_of(peer, chunk):
+        return slc.at[:, peer // halves, (peer % halves) * chunks + chunk]
 
     my_rows = pl.ds(pl.multiple_of(date * TILE, TILE), TILE)
-    pltpu.make_async_copy(tile_of(date), blocks.at[:, :, my_rows], sems.at[1]).start()
+    for chunk in range(chunks):
+        pltpu.make_async_copy(
+            tile_of(date, chunk), blocks.at[:, chunk, my_rows], sems.at[6 + chunk]
+        ).start()
 
     barrier = pltpu.get_barrier_semaphore()
     for step in range(1, dates):
@@ -59,16 +62,17 @@
         pl.semaphore_signal(barrier, inc=1, device_id=(date, other), device_id_type=MESH)
     pl.semaphore_wait(barrier, dates + 1)
 
-    for step in order:
-        peer = lax.rem(date + step, dates)
-        pltpu.make_async_remote_copy(
-            src_ref=tile_of(peer),
-            dst_ref=blocks.at[:, :, my_rows],
-            send_sem=sems.at[0],
-            recv_sem=sems.at[1],
-            device_id=(peer, col),
-            device_id_type=MESH,
-        ).start()
+    for chunk in range(chunks):
+        for step in order:
+            peer = lax.rem(date + step, dates)
+            pltpu.make_async_remote_copy(
+                src_ref=tile_of(peer, chunk),
+                dst_ref=blocks.at[:, chunk, my_rows],
+                send_sem=sems.at[0],
+                recv_sem=sems.at[6 + chunk],
+                device_id=(peer, col),
+                device_id_type=MESH,
+            ).start()
 
     looked_col = lax.broadcasted_iota(jnp.int32, (width, LANES), 0) // LOOK_COLS
     per_half = width // LOOK_COLS
@@ -87,36 +91,32 @@
         lane_off = jnp.where(mine, column, lane_off)
     chosen = [lane_off == o for o in range(1, MAX_OFFSET + 1)]
 
-    drain(blocks, sems.at[1])
-
     look_count = TILE // LOOK_ROWS
-    pieces = []
-    for look in range(look_count):
-        real_sums = [None] * MAX_OFFSET
-        imag_sums = [None] * MAX_OFFSET
-        power = None
-        for row in range(look * LOOK_ROWS, (look + 1) * LOOK_ROWS):
-            a0, a1 = [
-                jnp.concatenate(
-                    [
-                        blocks[comp, chunk, pl.ds(row, dates, stride=TILE), :]
-                        for chunk in range(chunks)
-                    ],
-                    axis=1,
-                )
-                for comp in range(2)
-            ]
-            squares = a0 * a0 + a1 * a1
-            power = squares if power is None else power + squares
-            for o in range(1, MAX_OFFSET + 1):
-                b0 = pltpu.roll(a0, dates - o, 0)
-                b1 = pltpu.roll(a1, dates - o, 0)
-                real = a0 * b0 + a1 * b1
-                imag = a1 * b0 - a0 * b1
-                real_sums[o - 1] = real if real_sums[o - 1] is None else real_sums[o - 1] + real
-                imag_sums[o - 1] = imag if imag_sums[o - 1] is None else imag_sums[o - 1] + imag
-        pieces += real_sums + imag_sums + [power]
-    pooled = split_dot(jnp.concatenate(pieces, axis=0), pool)
+    pooled = None
+    for chunk in range(chunks):
+        drain(blocks.at[:, chunk], sems.at[6 + chunk])
+        pieces = []
+        for look in range(look_count):
+            real_sums = [None] * MAX_OFFSET
+            imag_sums = [None] * MAX_OFFSET
+            power = None
+            for row in range(look * LOOK_ROWS, (look + 1) * LOOK_ROWS):
+                a0 = blocks[0, chunk, pl.ds(row, dates, stride=TILE), :]
+                a1 = blocks[1, chunk, pl.ds(row, dates, stride=TILE), :]
+                squares = a0 * a0 + a1 * a1
+                power = squares if power is None else power + squares
+                for o in range(MAX_OFFSET):
+                    b0 = pltpu.roll(a0, dates - 1 - o, 0)
+                    b1 = pltpu.roll(a1, dates - 1 - o, 0)
+                    real = a0 * b0 + a1 * b1
+                    imag = a1 * b0 - a0 * b1
+                    real_sums[o] = real if real_sums[o] is None else real_sums[o] + real
+                    imag_sums[o] = imag if imag_sums[o] is None else imag_sums[o] + imag
+            pieces += real_sums + imag_sums + [power]
+        part = split_dot(
+            jnp.concatenate(pieces, axis=0), pool[chunk * LANES : (chunk + 1) * LANES]
+        )
+        pooled = part if pooled is None else pooled + part
 
     count = 2 * MAX_OFFSET + 1
     for look in range(look_count):
@@ -152,7 +152,7 @@
             src_ref=tile,
             dst_ref=halo.at[half, spot],
             send_sem=sems.at[5],
-            recv_sem=sems.at[6],
+            recv_sem=sems.at[1],
             device_id=(peer, side),
             device_id_type=MESH,
         ).start()
@@ -165,7 +165,7 @@
     has_right = jnp.where(col < cols - 1, 1.0, 0.0)
 
     drain(landed, sems.at[3])
-    drain(halo, sems.at[6])
+    drain(halo, sems.at[1])
     sums = []
     for k in range(4):
         plane = pl.ds(k, look_rows, stride=4)
@@ -223,12 +223,15 @@
                 pltpu.VMEM((dates * TILE, LANES), jnp.float32),
                 pltpu.VMEM((halves, row_tiles * TILE, LANES), jnp.float32),
                 pltpu.VMEM((halves, row_tiles * TILE, LANES), jnp.float32),
-                pltpu.SemaphoreType.DMA((7,)),
+                pltpu.SemaphoreType.DMA((6 + width // LANES,)),
             ],
             compiler_params=pltpu.CompilerParams(
-                collective_id=0, has_side_effects=True, vmem_limit_bytes=55104 * 1024
+                collective_id=0, has_side_effects=True, vmem_limit_bytes=8 * 1024 * 1024
             ),
-        )(tiles, offsets.T)
+        )(
+            pltpu.with_memory_space_constraint(tiles, pltpu.HBM),
+            pltpu.with_memory_space_constraint(offsets.T, pltpu.HBM),
+        )
         return tuple(
             pl.pallas_call(
                 functools.partial(spread, slots),
@@ -236,6 +239,7 @@
                     jax.ShapeDtypeStruct((2, 1, slots, look_rows, cells), jnp.float32),
                     jax.ShapeDtypeStruct((1, slots, look_rows, cells), jnp.float32),
                 ),
+                compiler_params=pltpu.CompilerParams(vmem_limit_bytes=1024 * 1024),
             )(dense)
         )
 

time: 19.6 us -> 17.6 us (0.90)
  local copies, waits for them, and re-layouts: 1.27 us -> 0 us
  Pallas kernels: 17.5 us -> 16.8 us
    unnamed x4 -> x0, local copies, waits for them, and re-layouts: 1.27 us -> none
    pallas_call x1, Pallas kernels: 1.4 us -> 0.69 us  [shards(): pl.pallas_call(functools.partial(spread, slots), out_shape=(jax.ShapeDtyp...]
where the time goes in v3:
time: 17.6 us; the launch traced here: 17.4 us
  Pallas kernels  16.8 us (95%)
  between operations  0.64 us (4%)
    pallas_call x1, Pallas kernels, shards(): pl.pallas_call(functools.partial(kernel, dates, cols, slots), out_shape=j...  16.1 us
    pallas_call x1, Pallas kernels, shards(): pl.pallas_call(functools.partial(spread, slots), out_shape=(jax.ShapeDtyp...  0.69 us

profile of v3, /device:TPU:0, one launch (start us, length us, event | category | flops | bytes accessed | tf_op | source)
XLA Modules:
  0.0 17.4 jit_solution(18382847733159486288)
XLA Ops:
  0.6 16.1 %shard_map.41.dense = f32[3,8,128]{2,1,0:T(8,128)S(1)} custom-call(f32[2,4,4,8,128]{4,3,2,1,0:T(8,128)} %bitcast.4, s32[4,8]{1,0:T(4,128)} %bitcast.5), custom_call_target="tpu_custom_call" | custom-call | tf_op jit(solution)/shard_map/pallas_call | solution.py:215
  16.7 0.7 %shard_map.42 = (f32[2,1,4,8,32]{4,3,2,1,0:T(8,128)}, f32[1,4,8,32]{3,2,1,0:T(8,128)}) custom-call(f32[3,8,128]{2,1,0:T(8,128)S(1)} %shard_map.41.dense), custom_call_target="tpu_custom_call" | custom-call | tf_op jit(solution)/shard_map/pallas_call | solution.py:236

commit v4 on v3

--- a/solution.py
+++ b/solution.py
@@ -30,7 +30,7 @@
     return total
 
 
-def kernel(dates, cols, slots, slc, offsets, dense, blocks, offs, outbox, landed, halo, sems):
+def kernel(dates, cols, slots, slc, offsets, dense, blocks, offs, outbox, landed, halo, unfolded, sems):
     date, col = lax.axis_index("date"), lax.axis_index("col")
     chunks = blocks.shape[1]
     width = chunks * LANES
@@ -44,14 +44,11 @@
     offs_copy = pltpu.make_async_copy(offsets, offs, sems.at[4])
     offs_copy.start()
 
-    def tile_of(peer, chunk):
-        return slc.at[:, peer // halves, (peer % halves) * chunks + chunk]
+    def tile_of(peer):
+        return slc.at[:, peer // halves, pl.ds((peer % halves) * chunks, chunks)]
 
     my_rows = pl.ds(pl.multiple_of(date * TILE, TILE), TILE)
-    for chunk in range(chunks):
-        pltpu.make_async_copy(
-            tile_of(date, chunk), blocks.at[:, chunk, my_rows], sems.at[6 + chunk]
-        ).start()
+    pltpu.make_async_copy(tile_of(date), blocks.at[:, :, my_rows], sems.at[6]).start()
 
     barrier = pltpu.get_barrier_semaphore()
     for step in range(1, dates):
@@ -62,17 +59,16 @@
         pl.semaphore_signal(barrier, inc=1, device_id=(date, other), device_id_type=MESH)
     pl.semaphore_wait(barrier, dates + 1)
 
-    for chunk in range(chunks):
-        for step in order:
-            peer = lax.rem(date + step, dates)
-            pltpu.make_async_remote_copy(
-                src_ref=tile_of(peer, chunk),
-                dst_ref=blocks.at[:, chunk, my_rows],
-                send_sem=sems.at[0],
-                recv_sem=sems.at[6 + chunk],
-                device_id=(peer, col),
-                device_id_type=MESH,
-            ).start()
+    for step in order:
+        peer = lax.rem(date + step, dates)
+        pltpu.make_async_remote_copy(
+            src_ref=tile_of(peer),
+            dst_ref=blocks.at[:, :, my_rows],
+            send_sem=sems.at[0],
+            recv_sem=sems.at[6],
+            device_id=(peer, col),
+            device_id_type=MESH,
+        ).start()
 
     looked_col = lax.broadcasted_iota(jnp.int32, (width, LANES), 0) // LOOK_COLS
     per_half = width // LOOK_COLS
@@ -87,14 +83,14 @@
     for slot in range(slots):
         row = offs[slot : slot + 1, :].astype(jnp.float32)
         column = jnp.sum(jnp.where(eye, row, 0.0), axis=1, keepdims=True).astype(jnp.int32)
-        mine = (lane // cells == slot) & ((lane % cells) // per_half == half)
+        mine = lane // cells == slot
         lane_off = jnp.where(mine, column, lane_off)
     chosen = [lane_off == o for o in range(1, MAX_OFFSET + 1)]
 
     look_count = TILE // LOOK_ROWS
     pooled = None
+    drain(blocks, sems.at[6])
     for chunk in range(chunks):
-        drain(blocks.at[:, chunk], sems.at[6 + chunk])
         pieces = []
         for look in range(look_count):
             real_sums = [None] * MAX_OFFSET
@@ -119,45 +115,50 @@
         pooled = part if pooled is None else pooled + part
 
     count = 2 * MAX_OFFSET + 1
-    for look in range(look_count):
-        part = [
-            pooled[(look * count + q) * dates : (look * count + q + 1) * dates] for q in range(count)
-        ]
-        planes = [jnp.zeros((dates, LANES), jnp.float32) for _ in range(4)]
-        for o in range(1, MAX_OFFSET + 1):
-            take = chosen[o - 1]
-            planes[0] = jnp.where(take, part[o - 1], planes[0])
-            planes[1] = jnp.where(take, part[MAX_OFFSET + o - 1], planes[1])
-            planes[2] = jnp.where(take, part[2 * MAX_OFFSET], planes[2])
-            planes[3] = jnp.where(take, pltpu.roll(part[2 * MAX_OFFSET], dates - o, 0), planes[3])
-        for k in range(4):
-            outbox[pl.ds(look * 4 + k, dates, stride=TILE), :] = planes[k]
-
-    spot = pl.ds(pl.multiple_of(rt * TILE, TILE), TILE)
+    first = (lane % cells) // per_half == 0
+    part = [
+        jnp.where(
+            first,
+            pooled[q * dates : (q + 1) * dates],
+            pooled[(count + q) * dates : (count + q + 1) * dates],
+        )
+        for q in range(count)
+    ]
+    planes = [jnp.zeros((dates, LANES), jnp.float32) for _ in range(4)]
+    for o in range(1, MAX_OFFSET + 1):
+        take = chosen[o - 1]
+        planes[0] = jnp.where(take, part[o - 1], planes[0])
+        planes[1] = jnp.where(take, part[MAX_OFFSET + o - 1], planes[1])
+        planes[2] = jnp.where(take, part[2 * MAX_OFFSET], planes[2])
+        planes[3] = jnp.where(take, pltpu.roll(part[2 * MAX_OFFSET], dates - o, 0), planes[3])
+    for k in range(4):
+        outbox[:, k, :] = planes[k]
+
     for step in order + [0]:
         peer = lax.rem(date + step, dates)
-        tile = outbox.at[pl.ds(pl.multiple_of(peer * TILE, TILE), TILE)]
+        tile = outbox.at[peer]
         if step:
             pltpu.make_async_remote_copy(
                 src_ref=tile,
-                dst_ref=landed.at[half, spot],
+                dst_ref=landed.at[half, rt],
                 send_sem=sems.at[2],
                 recv_sem=sems.at[3],
                 device_id=(peer, col),
                 device_id_type=MESH,
             ).start()
         else:
-            pltpu.make_async_copy(tile, landed.at[half, spot], sems.at[3]).start()
+            pltpu.make_async_copy(tile, landed.at[half, rt], sems.at[3]).start()
         pltpu.make_async_remote_copy(
             src_ref=tile,
-            dst_ref=halo.at[half, spot],
+            dst_ref=halo.at[half, rt],
             send_sem=sems.at[5],
             recv_sem=sems.at[1],
             device_id=(peer, side),
             device_id_type=MESH,
         ).start()
 
-    look_rows = landed.shape[1] // 4
+    row_tiles = landed.shape[1]
+    look_rows = row_tiles * look_count
     lane = lax.broadcasted_iota(jnp.int32, (look_rows, LANES), 1) % cells
     line = lax.broadcasted_iota(jnp.int32, (look_rows, LANES), 0)
     left_edge, right_edge = lane == 0, lane == cells - 1
@@ -168,14 +169,22 @@
     drain(halo, sems.at[1])
     sums = []
     for k in range(4):
-        plane = pl.ds(k, look_rows, stride=4)
-        main = landed[0, plane, :]
-        for other in range(1, halves):
-            main = main + landed[other, plane, :]
+        ahead, behind = halo[0, :, k, :], halo[1, :, k, :]
+        near, far = landed[0, :, k, :], landed[1, :, k, :]
+        low = first[0:1]
+        expanded = (
+            (jnp.where(low, near, pltpu.roll(far, per_half, 1)), jnp.where(low, pltpu.roll(near, LANES - per_half, 1), far)),
+            (pltpu.roll(ahead, cells - 1, 1), pltpu.roll(ahead, per_half - 1, 1)),
+            (pltpu.roll(behind, LANES - per_half + 1, 1), pltpu.roll(behind, LANES - cells + 1, 1)),
+        )
+        for which in range(3):
+            for look in range(look_count):
+                unfolded[3 * k + which, pl.ds(look, row_tiles, stride=look_count), :] = expanded[which][look]
+        main = unfolded[3 * k]
         if k < 2:
             dense[k] = main
-        after = pltpu.roll(halo[0, plane, :], cells - 1, 1) * has_right
-        before = pltpu.roll(halo[halves - 1, plane, :], LANES - (cells - 1), 1) * has_left
+        after = unfolded[3 * k + 1] * has_right
+        before = unfolded[3 * k + 2] * has_left
         right = jnp.where(right_edge, after, pltpu.roll(main, LANES - 1, 1))
         left = jnp.where(left_edge, before, pltpu.roll(main, 1, 1))
         wide = main + left + right
@@ -186,7 +195,7 @@
     dense[2] = magnitude / (jnp.sqrt(sums[2] * sums[3]) + EPSILON)
 
     drain(blocks.at[:, :, pl.ds(0, (dates - 1) * TILE)], sems.at[0])
-    drain(outbox.at[pl.ds(0, (dates - 1) * TILE)], sems.at[2])
+    drain(outbox.at[pl.ds(0, dates - 1)], sems.at[2])
     drain(outbox, sems.at[5])
 
 
@@ -220,10 +229,11 @@
             scratch_shapes=[
                 pltpu.VMEM((2, width // LANES, dates * TILE, LANES), jnp.float32),
                 pltpu.VMEM((slots, dates), jnp.int32),
-                pltpu.VMEM((dates * TILE, LANES), jnp.float32),
-                pltpu.VMEM((halves, row_tiles * TILE, LANES), jnp.float32),
-                pltpu.VMEM((halves, row_tiles * TILE, LANES), jnp.float32),
-                pltpu.SemaphoreType.DMA((6 + width // LANES,)),
+                pltpu.VMEM((dates, 4, LANES), jnp.float32),
+                pltpu.VMEM((halves, row_tiles, 4, LANES), jnp.float32),
+                pltpu.VMEM((halves, row_tiles, 4, LANES), jnp.float32),
+                pltpu.VMEM((12, look_rows, LANES), jnp.float32),
+                pltpu.SemaphoreType.DMA((7,)),
             ],
             compiler_params=pltpu.CompilerParams(
                 collective_id=0, has_side_effects=True, vmem_limit_bytes=8 * 1024 * 1024

time: 17.6 us -> 17.5 us (level)
  no operation moved by 1% of the time
where the time goes in v4:
time: 17.5 us; the launch traced here: 17.4 us
  Pallas kernels  16.7 us (95%)
  between operations  0.64 us (4%)
    pallas_call x1, Pallas kernels, shards(): pl.pallas_call(functools.partial(kernel, dates, cols, slots), out_shape=j...  16 us
    pallas_call x1, Pallas kernels, shards(): pl.pallas_call(functools.partial(spread, slots), out_shape=(jax.ShapeDtyp...  0.69 us

profile of v4, /device:TPU:0, one launch (start us, length us, event | category | flops | bytes accessed | tf_op | source)
XLA Modules:
  0.0 17.4 jit_solution(16597976977160739005)
XLA Ops:
  0.6 16.0 %shard_map.41.dense = f32[3,8,128]{2,1,0:T(8,128)S(1)} custom-call(f32[2,4,4,8,128]{4,3,2,1,0:T(8,128)} %bitcast.4, s32[4,8]{1,0:T(4,128)} %bitcast.5), custom_call_target="tpu_custom_call" | custom-call | tf_op jit(solution)/shard_map/pallas_call | solution.py:224
  16.7 0.7 %shard_map.42 = (f32[2,1,4,8,32]{4,3,2,1,0:T(8,128)}, f32[1,4,8,32]{3,2,1,0:T(8,128)}) custom-call(f32[3,8,128]{2,1,0:T(8,128)S(1)} %shard_map.41.dense), custom_call_target="tpu_custom_call" | custom-call | tf_op jit(solution)/shard_map/pallas_call | solution.py:246

commit v5 on v4

--- a/solution.py
+++ b/solution.py
@@ -30,7 +30,7 @@
     return total
 
 
-def kernel(dates, cols, slots, slc, offsets, dense, blocks, offs, outbox, landed, halo, unfolded, sems):
+def kernel(dates, cols, slots, slc, offsets, dense, blocks, offs, outbox, landed, halo, unfolded, staged, sems):
     date, col = lax.axis_index("date"), lax.axis_index("col")
     chunks = blocks.shape[1]
     width = chunks * LANES
@@ -44,11 +44,14 @@
     offs_copy = pltpu.make_async_copy(offsets, offs, sems.at[4])
     offs_copy.start()
 
-    def tile_of(peer):
-        return slc.at[:, peer // halves, pl.ds((peer % halves) * chunks, chunks)]
+    stage_copy = pltpu.make_async_copy(slc, staged, sems.at[7])
+    stage_copy.start()
+
+    def tile_of(source, peer):
+        return source.at[:, peer // halves, pl.ds((peer % halves) * chunks, chunks)]
 
     my_rows = pl.ds(pl.multiple_of(date * TILE, TILE), TILE)
-    pltpu.make_async_copy(tile_of(date), blocks.at[:, :, my_rows], sems.at[6]).start()
+    pltpu.make_async_copy(tile_of(slc, date), blocks.at[:, :, my_rows], sems.at[6]).start()
 
     barrier = pltpu.get_barrier_semaphore()
     for step in range(1, dates):
@@ -58,11 +61,12 @@
         other = lax.rem(col + step, cols)
         pl.semaphore_signal(barrier, inc=1, device_id=(date, other), device_id_type=MESH)
     pl.semaphore_wait(barrier, dates + 1)
+    stage_copy.wait()
 
     for step in order:
         peer = lax.rem(date + step, dates)
         pltpu.make_async_remote_copy(
-            src_ref=tile_of(peer),
+            src_ref=tile_of(staged, peer),
             dst_ref=blocks.at[:, :, my_rows],
             send_sem=sems.at[0],
             recv_sem=sems.at[6],
@@ -233,7 +237,8 @@
                 pltpu.VMEM((halves, row_tiles, 4, LANES), jnp.float32),
                 pltpu.VMEM((halves, row_tiles, 4, LANES), jnp.float32),
                 pltpu.VMEM((12, look_rows, LANES), jnp.float32),
-                pltpu.SemaphoreType.DMA((7,)),
+                pltpu.VMEM(tiles.shape, jnp.float32),
+                pltpu.SemaphoreType.DMA((8,)),
             ],
             compiler_params=pltpu.CompilerParams(
                 collective_id=0, has_side_effects=True, vmem_limit_bytes=8 * 1024 * 1024

time: 17.5 us -> 17.3 us (0.989)
  Pallas kernels: 16.7 us -> 16.5 us
    pallas_call x1, Pallas kernels: 16 us -> 15.8 us  [shards(): pl.pallas_call(functools.partial(kernel, dates, cols, slots), out_shape=j...]
where the time goes in v5:
time: 17.3 us; the launch traced here: 17.2 us
  Pallas kernels  16.5 us (95%)
  between operations  0.64 us (4%)
    pallas_call x1, Pallas kernels, shards(): pl.pallas_call(functools.partial(kernel, dates, cols, slots), out_shape=j...  15.8 us
    pallas_call x1, Pallas kernels, shards(): pl.pallas_call(functools.partial(spread, slots), out_shape=(jax.ShapeDtyp...  0.69 us

profile of v5, /device:TPU:0, one launch (start us, length us, event | category | flops | bytes accessed | tf_op | source)
XLA Modules:
  0.0 17.2 jit_solution(9517510503556124604)
XLA Ops:
  0.6 15.8 %shard_map.41.dense = f32[3,8,128]{2,1,0:T(8,128)S(1)} custom-call(f32[2,4,4,8,128]{4,3,2,1,0:T(8,128)} %bitcast.4, s32[4,8]{1,0:T(4,128)} %bitcast.5), custom_call_target="tpu_custom_call" | custom-call | tf_op jit(solution)/shard_map/pallas_call | solution.py:228
  16.5 0.7 %shard_map.42 = (f32[2,1,4,8,32]{4,3,2,1,0:T(8,128)}, f32[1,4,8,32]{3,2,1,0:T(8,128)}) custom-call(f32[3,8,128]{2,1,0:T(8,128)S(1)} %shard_map.41.dense), custom_call_target="tpu_custom_call" | custom-call | tf_op jit(solution)/shard_map/pallas_call | solution.py:251

commit v6 on v5

--- a/solution.py
+++ b/solution.py
@@ -41,25 +41,26 @@
 
     order = sorted(range(1, dates), key=lambda step: abs(2 * step - dates))
 
-    offs_copy = pltpu.make_async_copy(offsets, offs, sems.at[4])
-    offs_copy.start()
-
-    stage_copy = pltpu.make_async_copy(slc, staged, sems.at[7])
-    stage_copy.start()
-
-    def tile_of(source, peer):
-        return source.at[:, peer // halves, pl.ds((peer % halves) * chunks, chunks)]
-
-    my_rows = pl.ds(pl.multiple_of(date * TILE, TILE), TILE)
-    pltpu.make_async_copy(tile_of(slc, date), blocks.at[:, :, my_rows], sems.at[6]).start()
-
     barrier = pltpu.get_barrier_semaphore()
-    for step in range(1, dates):
+    for step in order:
         peer = lax.rem(date + step, dates)
         pl.semaphore_signal(barrier, inc=1, device_id=(peer, col), device_id_type=MESH)
     for step in (1, cols - 1):
         other = lax.rem(col + step, cols)
         pl.semaphore_signal(barrier, inc=1, device_id=(date, other), device_id_type=MESH)
+
+    offs_copy = pltpu.make_async_copy(offsets, offs, sems.at[4])
+    offs_copy.start()
+
+    stage_copy = pltpu.make_async_copy(slc, staged, sems.at[7])
+    stage_copy.start()
+
+    def tile_of(source, peer):
+        return source.at[:, peer // halves, pl.ds((peer % halves) * chunks, chunks)]
+
+    my_rows = pl.ds(pl.multiple_of(date * TILE, TILE), TILE)
+    pltpu.make_async_copy(tile_of(slc, date), blocks.at[:, :, my_rows], sems.at[6]).start()
+
     pl.semaphore_wait(barrier, dates + 1)
     stage_copy.wait()
 

time: 17.3 us -> 17.4 us (level)
  no operation moved by 1% of the time
where the time goes in v6:
time: 17.4 us; the launch traced here: 17.2 us
  Pallas kernels  16.6 us (95%)
  between operations  0.64 us (4%)
    pallas_call x1, Pallas kernels, shards(): pl.pallas_call(functools.partial(kernel, dates, cols, slots), out_shape=j...  15.9 us
    pallas_call x1, Pallas kernels, shards(): pl.pallas_call(functools.partial(spread, slots), out_shape=(jax.ShapeDtyp...  0.69 us

profile of v6, /device:TPU:0, one launch (start us, length us, event | category | flops | bytes accessed | tf_op | source)
XLA Modules:
  0.0 17.2 jit_solution(2476737346868822851)
XLA Ops:
  0.6 15.9 %shard_map.41.dense = f32[3,8,128]{2,1,0:T(8,128)S(1)} custom-call(f32[2,4,4,8,128]{4,3,2,1,0:T(8,128)} %bitcast.4, s32[4,8]{1,0:T(4,128)} %bitcast.5), custom_call_target="tpu_custom_call" | custom-call | tf_op jit(solution)/shard_map/pallas_call | solution.py:229
  16.5 0.7 %shard_map.42 = (f32[2,1,4,8,32]{4,3,2,1,0:T(8,128)}, f32[1,4,8,32]{3,2,1,0:T(8,128)}) custom-call(f32[3,8,128]{2,1,0:T(8,128)S(1)} %shard_map.41.dense), custom_call_target="tpu_custom_call" | custom-call | tf_op jit(solution)/shard_map/pallas_call | solution.py:252
